TPU v7x, 256 devices: a whole 4x4x8 slice. The times are simulated.
256 devices in a mesh: space: 8 (over z_hi, y), dp: 32 (over x, z_lo, core).
Axes of the slice: x: 4, y: 4, z: 8 (z_hi: 2, z_lo: 4; z = z_hi * 4 + z_lo), core: 2. Of those that a mesh axis runs over, the one named last changes fastest.
Arguments:
- features: bfloat16 [32, 48, 64, 8, 128], P('dp', None, 'space'), may hold values from -21 to 21
- upstream: bfloat16 [32, 48, 64, 8, 128], P('dp', None, 'space'), may hold values from -21 to 21
- weight_one: bfloat16 [48, 48, 3, 3, 3], replicated, may hold values from -0.15625 to 0.15625
- weight_two: bfloat16 [48, 48, 3, 3, 3], replicated, may hold values from -0.15625 to 0.15625
- norm_gain: float32 [48], replicated, may hold values from 0.25 to 1.75
- norm_bias: float32 [48], replicated, may hold values from -3 to 3
Outputs:
- grad_input: bfloat16 [32, 48, 64, 8, 128], P('dp', None, 'space')
- grad_one: float32 [48, 48, 3, 3, 3], replicated
- grad_two: float32 [48, 48, 3, 3, 3], replicated
- grad_gain: float32 [48], replicated
- grad_bias: float32 [48], replicated
All inputs are finite; a program needn't handle non-finite values.
Results may differ from a plain program's by a relative error of at most 0.0029.
Values may be sent and summed in bfloat16 or wider, within the bound.
A program may use at most 128 MiB of HBM per device.

v0:
```python
import jax
import jax.numpy as jnp
from jax import lax
from jax.sharding import PartitionSpec as P

epsilon = 1e-05


def padded_2(cells, sides, width):
    for axis, dim in sides:
        count = lax.axis_size(axis)
        ends = count - 1
        head = lax.slice_in_dim(cells, 0, width, axis=dim)
        tail = lax.slice_in_dim(cells, cells.shape[dim] - width, cells.shape[dim], axis=dim)
        cells = jnp.concatenate(
            [
                lax.ppermute(tail, axis, [(i, (i + 1) % count) for i in range(ends)]),
                cells,
                lax.ppermute(head, axis, [((i + 1) % count, i) for i in range(ends)]),
            ],
            axis=dim,
        )
    return cells


def slab_faces(field):
    return padded_2(field, (("space", 2),), 1)


def conv_slab(padded, kernel):
    return lax.conv_general_dilated(
        padded,
        kernel,
        (1, 1, 1),
        ((0, 0), (1, 1), (1, 1)),
        dimension_numbers=("NCDHW", "OIDHW", "NCDHW"),
        preferred_element_type=jnp.float32,
    )


def flipped(kernel):
    return jnp.transpose(kernel, (1, 0, 2, 3, 4))[:, :, ::-1, ::-1, ::-1]


def kernel_grad(padded, target):
    return lax.conv_general_dilated(
        padded,
        target,
        (1, 1, 1),
        ((0, 0), (1, 1), (1, 1)),
        dimension_numbers=("CNDHW", "IODHW", "CNDHW"),
        preferred_element_type=jnp.float32,
    )


def local(features, upstream, weight_one, weight_two, norm_gain, norm_bias):
    axes_cells = (2, 3, 4)
    cells_all = float(
        features.shape[2] * features.shape[3] * features.shape[4] * lax.axis_size("space")
    )
    padded_x = slab_faces(features)
    pre_act = conv_slab(padded_x, weight_one)
    sums_pre, squares_pre = lax.psum(
        (
            jnp.sum(pre_act, axis=axes_cells, keepdims=True),
            jnp.sum(pre_act * pre_act, axis=axes_cells, keepdims=True),
        ),
        "space",
    )
    mean_pre = sums_pre / cells_all
    inv_std = lax.rsqrt(squares_pre / cells_all - mean_pre * mean_pre + epsilon)
    normal_hat = (pre_act - mean_pre) * inv_std
    gain_b = norm_gain.reshape(1, -1, 1, 1, 1)
    normed = normal_hat * gain_b + norm_bias.reshape(1, -1, 1, 1, 1)
    sigmoid_val = jax.nn.sigmoid(normed)
    hidden = (normed * sigmoid_val).astype(jnp.bfloat16)
    padded_h = slab_faces(hidden)
    padded_g = slab_faces(upstream)
    local_two = kernel_grad(padded_h, upstream)
    grad_hidden = conv_slab(padded_g, flipped(weight_two))
    grad_norm = grad_hidden * sigmoid_val * (1.0 + normed * (1.0 - sigmoid_val))
    local_bias = jnp.sum(grad_norm, axis=(0, 2, 3, 4))
    local_gain = jnp.sum(grad_norm * normal_hat, axis=(0, 2, 3, 4))
    slope_sum, slope_dot = lax.psum(
        (
            jnp.sum(grad_norm, axis=axes_cells, keepdims=True),
            jnp.sum(grad_norm * normal_hat, axis=axes_cells, keepdims=True),
        ),
        "space",
    )
    grad_pre = (
        gain_b
        * inv_std
        * (grad_norm - slope_sum / cells_all - normal_hat * (slope_dot / cells_all))
    ).astype(jnp.bfloat16)
    padded_grad = slab_faces(grad_pre)
    local_one = kernel_grad(padded_x, grad_pre)
    back = conv_slab(padded_grad, flipped(weight_one))
    grad_input = (upstream.astype(jnp.float32) + back).astype(jnp.bfloat16)
    grad_one, grad_two, grad_gain, grad_bias = lax.psum(
        (local_one, local_two, local_gain, local_bias), ("space", "dp")
    )
    return (grad_input, grad_one, grad_two, grad_gain, grad_bias)


def solution(mesh):
    in_specs = (
        P("dp", None, "space", None, None),
        P("dp", None, "space", None, None),
        P(),
        P(),
        P(),
        P(),
    )
    out_specs = (P("dp", None, "space", None, None), P(), P(), P(), P())
    return jax.shard_map(local, mesh=mesh, in_specs=in_specs, out_specs=out_specs, check_vma=False)
```

profile of v0, /device:TPU:1, one launch (start us, length us, event | category | flops | bytes accessed | tf_op | source)
XLA Modules:
  0.0 684.3 jit_solution(1534281291638809892)
XLA Ops:
  7.2 1.0 fusion.73
  8.3 4.2 collective-permute-start
  12.5 1.3 collective-permute-start.1
  13.8 1.6 fusion.74
  15.4 4.6 collective-permute-start.2
  20.0 1.3 collective-permute-start.3
  21.3 7.4 %copy.112 = bf16[1,48,8,8,128]{1,0,4,3,2:T(2,128)(2,1)} copy(bf16[1,48,8,8,128]{4,3,2,1,0:T(8,128)(2,1)} %param.7) | data formatting | bytes 1572864 | tf_op args[1]
  28.7 2.5 copy.85
  31.3 3.5 copy.86
  34.8 3.6 fusion.70
  38.4 3.1 fusion.68
  42.1 1.5 copy-done.10
  43.6 0.8 slice.50
  44.4 2.0 pad_maximum_fusion.3
  46.5 4.9 copy.89
  51.3 2.3 pad.2
  53.7 0.5 copy.91
  54.2 0.8 slice.51
  55.0 1.2 copy-done.11
  56.6 12.1 %select_reduce_fusion.3 = (f32[48]{0:T(128)S(1)}, f32[48]{0:T(128)S(1)}, f32[8,8,8,17,48]{4,2,3,1,0:T(8,128)}) fusion(pred[8,17]{0,1:T(8,128)(4,1)S(1)} %copy-done.14, bf16[48,48,3,3,3]{1,0,4,3,2:T(8,128)(2,1)S(1)} %copy-done, bf16[48,10,8,1,7,2]{0,4,5,2,1,3:T(8,128)(2,1)S(1)} %copy-done.13, bf16[48,10,8,1,8,17]{0,4,5,2,1,3:T(8,128)(2,1)S(1)} %copy-done.11), kind=kOutput, calls=%fused_computation.25 | convolution fusion | flops 998682496 | bytes 2948104 | tf_op jit(solution)/shard_map/conv_general_dilated | solution.py:31
  68.7 30.8 %all-reduce.3 = (f32[1,48,1,1,1]{1,4,3,2,0:T(1,128)S(1)}, f32[1,48,1,1,1]{1,4,3,2,0:T(1,128)S(1)}) all-reduce(f32[1,48,1,1,1]{1,4,3,2,0:T(1,128)S(1)} %bitcast.113, f32[1,48,1,1,1]{1,4,3,2,0:T(1,128)S(1)} %bitcast.112), channel_id=1, replica_groups=mesh['space'=8,'dp'=32] {'space'}, use_global_device_ids=true, to_apply=%region_1.0 | all-reduce | flops 96 | bytes 768 | tf_op jit(solution)/shard_map/psum | solution.py:63
  99.5 16.4 %select_reduce_fusion = (f32[48]{0:T(128)S(1)}, f32[48]{0:T(128)S(1)}, f32[8,8,8,17,48]{4,2,3,1,0:T(8,128)}) fusion(pred[8,17]{0,1:T(8,128)(4,1)S(1)} %copy-done.14, f32[48]{0:T(128)S(1)} %bitcast.108, f32[48]{0:T(128)S(1)} %get-tuple-element.55, f32[8,8,8,17,48]{4,2,3,1,0:T(8,128)} %get-tuple-element.56, f32[48]{0:T(128)S(1)} %copy-done.16, ...), kind=kOutput, calls=%fused_computation.17 | convolution fusion | flops 1004113792 | bytes 4620040 | tf_op jit(solution)/shard_map/conv_general_dilated | solution.py:31
  115.9 25.0 %all-reduce.2 = (f32[1,48,1,1,1]{1,4,3,2,0:T(1,128)S(1)}, f32[1,48,1,1,1]{1,4,3,2,0:T(1,128)S(1)}) all-reduce(f32[1,48,1,1,1]{1,4,3,2,0:T(1,128)S(1)} %bitcast.111, f32[1,48,1,1,1]{1,4,3,2,0:T(1,128)S(1)} %bitcast.110), channel_id=1, replica_groups=mesh['space'=8,'dp'=32] {'space'}, use_global_device_ids=true, to_apply=%region_5.0 | all-reduce | flops 96 | bytes 768 | tf_op jit(solution)/shard_map/psum | solution.py:84
  140.9 4.9 multiply_convert_fusion.1
  146.3 1.2 copy.128
  147.5 2.2 collective-permute-start.6
  149.8 1.2 copy.127
  151.0 1.3 collective-permute-start.7
  152.3 2.3 copy.117
  154.6 2.3 copy.118
  156.9 1.9 copy.104
  159.0 4.0 collective-permute-start.4
  163.0 1.3 collective-permute-start.5
  164.3 1.5 fusion.36
  165.9 17.9 %fusion.49 = f32[48,48,3,3,3]{0,1,4,3,2:T(8,128)} fusion(bf16[8,8,8,17,48]{4,2,3,1,0:T(8,128)(2,1)S(1)} %get-tuple-element.40, pred[8,17]{0,1:T(8,128)(4,1)S(1)} %copy-done.14, bf16[48,10,8,8,17,1]{0,3,5,4,2,1:T(8,128)(2,1)S(1)} %get-tuple-element.60, bf16[48,10,8,8,17,1]{0,3,5,4,2,1:T(8,128)(2,1)} %copy.104, ...), kind=kOutput, calls=%fused_computation.61 | convolution fusion | flops 1002491904 | bytes 4217992 | tf_op jit(solution)/shard_map/conv_general_dilated | solution.py:46
  184.3 6.4 copy.126
  190.7 101.2 %all-reduce = (f32[48]{0:T(128)}, f32[48]{0:T(128)}) all-reduce(f32[48]{0:T(128)S(1)} %get-tuple-element.25, f32[48]{0:T(128)S(1)} %get-tuple-element.26), channel_id=1, replica_groups=mesh['space'=8,'dp'=32] {'space','dp'}, use_global_device_ids=true, to_apply=%region_10.0 | all-reduce | flops 96 | bytes 768 | tf_op jit(solution)/shard_map/psum | solution.py:100
  291.9 0.6 maximum_bitcast_fusion
  292.5 0.6 pad.7
  293.7 10.5 %broadcast_select_fusion = f32[8,8,8,17,48]{4,2,3,1,0:T(8,128)S(1)} fusion(pred[8,17]{0,1:T(8,128)(4,1)S(1)} %copy-done.14, bf16[48,48,3,3,3]{1,0,4,3,2:T(8,128)(2,1)S(1)} %copy-done, bf16[48,10,8,1,7,2]{0,4,5,2,1,3:T(8,128)(2,1)S(1)} %slice.57, bf16[48,10,8,1,8,17]{0,4,5,2,1,3:T(8,128)(2,1)S(1)} %copy.98), kind=kOutput, calls=%fused_computation.55 | convolution fusion | flops 996593664 | bytes 2947720 | tf_op jit(solution)/shard_map/conv_general_dilated | solution.py:31
  304.2 3.1 copy.99
  307.4 1.8 copy-done.8
  309.3 110.6 %fusion.11 = f32[48,48,3,3,3]{0,1,4,3,2:T(8,128)} fusion(bf16[1,48,8,8,128]{1,0,4,3,2:T(2,128)(2,1)S(1)} %copy-done.7, bf16[1,48,1,8,128]{1,0,4,3,2:T(2,128)(2,1)} %collective-permute-done.7, bf16[1,48,8,8,128]{1,0,4,3,2:T(2,128)(2,1)S(1)} %bitcast.102, bf16[1,48,1,8,128]{1,0,4,3,2:T(2,128)(2,1)} %collective-permute-done.6), kind=kOutput, calls=%fused_computation.15 | convolution fusion | flops 932364288 | bytes 2018304 | tf_op jit(solution)/shard_map/conv_general_dilated | solution.py:46
  419.9 4.1 fusion.13
  424.0 3.8 copy.113
  427.8 245.1 %all-reduce.6.cloned.1.call-done = (f32[48,48,3,3,3]{0,1,4,3,2:T(8,128)}, f32[48,48,3,3,3]{0,1,4,3,2:T(8,128)}) async-done(((f32[48,48,3,3,3]{0,1,4,3,2:T(8,128)}, f32[48,48,3,3,3]{0,1,4,3,2:T(8,128)}), (f32[48,48,3,3,3]{0,1,4,3,2:T(8,128)}, f32[48,48,3,3,3]{0,1,4,3,2:T(8,128)})) %all-reduce.6.cloned.1.call-update) | async-done | bytes 497680 | tf_op jit(solution)/shard_map/psum | solution.py:100
  672.9 2.2 copy.114
  675.1 2.2 copy.115
  (64 shorter events, 3.1 us)
Async XLA Ops:
  7.2 47.9 %copy-start = (bf16[48,48,3,3,3]{1,0,4,3,2:T(8,128)(2,1)S(1)}, bf16[48,48,3,3,3]{1,0,4,3,2:T(8,128)(2,1)}, u32[]{:S(2)}) copy-start(bf16[48,48,3,3,3]{1,0,4,3,2:T(8,128)(2,1)} %param.8) | copy-start | bytes 373252
  7.2 21.5 %copy-start.5 = (bf16[1,48,8,8,128]{4,3,2,1,0:T(8,128)(2,1)S(1)}, bf16[1,48,8,8,128]{4,3,2,1,0:T(8,128)(2,1)}, u32[]{:S(2)}) copy-start(bf16[1,48,8,8,128]{4,3,2,1,0:T(8,128)(2,1)} %param.7) | copy-start | bytes 2359300
  7.2 665.7 %all-reduce.6.cloned.1.call-start = ((), (), s32[]{:S(2)}) async-start(), calls=%async_computation | async-start | bytes 2654208 | tf_op jit(solution)/shard_map/psum | solution.py:100
  8.3 22.9 %copy-start.12 = (bf16[1,48,8,8,128]{4,3,2,1,0:T(8,128)(2,1)S(1)}, bf16[1,48,8,8,128]{4,3,2,1,0:T(8,128)(2,1)}, u32[]{:S(2)}) copy-start(bf16[1,48,8,8,128]{4,3,2,1,0:T(8,128)(2,1)} %param.6) | copy-start | bytes 2359300
  8.3 22.9 %collective-permute-start = (bf16[1,48,1,8,128]{4,3,2,1,0:T(8,128)(2,1)S(1)}, bf16[1,48,1,8,128]{4,3,2,1,0:T(8,128)(2,1)S(1)}, u32[]{:S(2)}, u32[]{:S(2)}) collective-permute-start(bf16[1,48,1,8,128]{4,3,2,1,0:T(8,128)(2,1)S(1)} %get-tuple-element.51), channel_id=1, source_target_pairs={{0,32},{32,64},{64,96},{96,128},{128,160},{160,192},{192,224},{1,3... | collective-permute-start | bytes 294920 | tf_op jit(solution)/shard_map/ppermute | solution.py:17
  12.5 18.7 %collective-permute-start.1 = (bf16[1,48,1,8,128]{4,3,2,1,0:T(8,128)(2,1)S(1)}, bf16[1,48,1,8,128]{4,3,2,1,0:T(8,128)(2,1)S(1)}, u32[]{:S(2)}, u32[]{:S(2)}) collective-permute-start(bf16[1,48,1,8,128]{4,3,2,1,0:T(8,128)(2,1)S(1)} %get-tuple-element.52), channel_id=1, source_target_pairs={{32,0},{64,32},{96,64},{128,96},{160,128},{192,160},{224,192},{33,... | collective-permute-start | bytes 294920 | tf_op jit(solution)/shard_map/ppermute | solution.py:19
  15.4 29.1 %collective-permute-start.2 = (bf16[1,48,1,8,128]{4,3,2,1,0:T(8,128)(2,1)}, bf16[1,48,1,8,128]{4,3,2,1,0:T(8,128)(2,1)}, u32[]{:S(2)}, u32[]{:S(2)}) collective-permute-start(bf16[1,48,1,8,128]{4,3,2,1,0:T(8,128)(2,1)} %get-tuple-element.53), channel_id=1, source_target_pairs={{0,32},{32,64},{64,96},{96,128},{128,160},{160,192},{192,224},{1,3... | collective-permute-start | bytes 294920 | tf_op jit(solution)/shard_map/ppermute | solution.py:17
  20.0 24.4 %collective-permute-start.3 = (bf16[1,48,1,8,128]{4,3,2,1,0:T(8,128)(2,1)S(1)}, bf16[1,48,1,8,128]{4,3,2,1,0:T(8,128)(2,1)}, u32[]{:S(2)}, u32[]{:S(2)}) collective-permute-start(bf16[1,48,1,8,128]{4,3,2,1,0:T(8,128)(2,1)S(1)} %get-tuple-element.54), channel_id=1, source_target_pairs={{32,0},{64,32},{96,64},{128,96},{160,128},{192,160},{224,192},{33,... | collective-permute-start | bytes 294920 | tf_op jit(solution)/shard_map/ppermute | solution.py:19
  41.5 2.9 copy-start.6
  42.1 1.6 copy-start.10
  53.7 2.6 copy-start.11
  53.7 2.8 copy-start.13
  53.7 2.8 copy-start.14
  54.2 14.5 %copy-start.9 = (bf16[48,10,8,1,8,17]{0,4,5,2,1,3:T(8,128)(2,1)}, bf16[48,10,8,1,8,17]{0,4,5,2,1,3:T(8,128)(2,1)S(1)}, u32[]{:S(2)}) copy-start(bf16[48,10,8,1,8,17]{0,4,5,2,1,3:T(8,128)(2,1)S(1)} %copy.91) | copy-start | bytes 3133444
  56.5 43.0 %copy-start.15 = (f32[48]{0:T(128)S(1)}, f32[48]{0:T(128)}, u32[]{:S(2)}) copy-start(f32[48]{0:T(128)} %param.10) | copy-start | bytes 580
  56.5 43.0 %copy-start.16 = (f32[48]{0:T(128)S(1)}, f32[48]{0:T(128)}, u32[]{:S(2)}) copy-start(f32[48]{0:T(128)} %param.11) | copy-start | bytes 580
  145.8 6.5 copy-start.3
  146.2 8.3 %copy-start.2 = (bf16[48,10,8,1,8,16]{0,2,5,4,1,3:T(8,128)(2,1)S(1)}, bf16[48,10,8,1,8,16]{0,2,5,4,1,3:T(8,128)(2,1)}, u32[]{:S(2)}) copy-start(bf16[48,10,8,1,8,16]{0,2,5,4,1,3:T(8,128)(2,1)} %get-tuple-element.42) | copy-start | bytes 2949124
  147.5 159.8 %collective-permute-start.6 = (bf16[1,48,1,8,128]{1,0,4,3,2:T(2,128)(2,1)}, bf16[1,48,1,8,128]{1,0,4,3,2:T(2,128)(2,1)}, u32[]{:S(2)}, u32[]{:S(2)}) collective-permute-start(bf16[1,48,1,8,128]{1,0,4,3,2:T(2,128)(2,1)} %bitcast.90), channel_id=1, source_target_pairs={{0,32},{32,64},{64,96},{96,128},{128,160},{160,192},{192,224},{1,3... | collective-permute-start | bytes 294920 | tf_op jit(solution)/shard_map/ppermute | solution.py:17
  151.0 156.3 %collective-permute-start.7 = (bf16[1,48,1,8,128]{1,0,4,3,2:T(2,128)(2,1)}, bf16[1,48,1,8,128]{1,0,4,3,2:T(2,128)(2,1)}, u32[]{:S(2)}, u32[]{:S(2)}) collective-permute-start(bf16[1,48,1,8,128]{1,0,4,3,2:T(2,128)(2,1)} %bitcast.89), channel_id=1, source_target_pairs={{32,0},{64,32},{96,64},{128,96},{160,128},{192,160},{224,192},{33,... | collective-permute-start | bytes 294920 | tf_op jit(solution)/shard_map/ppermute | solution.py:19
  159.0 132.9 %collective-permute-start.4 = (bf16[1,48,1,8,128]{1,3,4,0,2:T(8,128)(2,1)S(1)}, bf16[1,48,1,8,128]{1,3,4,0,2:T(8,128)(2,1)S(1)}, u32[]{:S(2)}, u32[]{:S(2)}) collective-permute-start(bf16[1,48,1,8,128]{1,3,4,0,2:T(8,128)(2,1)S(1)} %slice_bitcast_fusion.3), channel_id=1, source_target_pairs={{0,32},{32,64},{64,96},{96,128},{128,160},{160,192},{192,224},{1,3... | collective-permute-start | bytes 294920 | tf_op jit(solution)/shard_map/ppermute | solution.py:17
  163.0 128.9 %collective-permute-start.5 = (bf16[1,48,1,8,128]{1,3,4,2,0:T(8,128)(2,1)S(1)}, bf16[1,48,1,8,128]{1,3,4,2,0:T(8,128)(2,1)S(1)}, u32[]{:S(2)}, u32[]{:S(2)}) collective-permute-start(bf16[1,48,1,8,128]{1,3,4,2,0:T(8,128)(2,1)S(1)} %slice_bitcast_fusion.2), channel_id=1, source_target_pairs={{32,0},{64,32},{96,64},{128,96},{160,128},{192,160},{224,192},{33,... | collective-permute-start | bytes 294920 | tf_op jit(solution)/shard_map/ppermute | solution.py:19
  304.2 3.3 copy-start.7
  304.2 5.1 copy-start.8
  309.2 110.6 %copy-start.4 = (bf16[1,48,8,8,128]{1,3,4,2,0:T(8,128)(2,1)S(1)}, bf16[1,48,8,8,128]{1,3,4,2,0:T(8,128)(2,1)}, u32[]{:S(2)}) copy-start(bf16[1,48,8,8,128]{1,3,4,2,0:T(8,128)(2,1)} %copy.85) | copy-start | bytes 2359300
  419.9 257.4 %copy-start.1 = (bf16[48,48,3,3,3]{1,0,4,3,2:T(8,128)(2,1)S(1)}, bf16[48,48,3,3,3]{1,0,4,3,2:T(8,128)(2,1)}, u32[]{:S(2)}) copy-start(bf16[48,48,3,3,3]{1,0,4,3,2:T(8,128)(2,1)} %param.8) | copy-start | bytes 373252
Sparse Core Ops, SparseCore 0:
  420.0 252.9 all-reduce.5
where the time goes:
time: 690 us; the launch traced here: 684 us
  waiting for transfers between devices  245 us (36%)
  matrix products  167 us (24%)
  blocking collectives  157 us (23%)
  local copies, waits for them, and re-layouts  66.6 us (10%)
  starting transfers between devices  20.2 us (3%)
  between operations  14.7 us (2%)
  other arithmetic  13.3 us (2%)
    psum x1, waiting for transfers between devices, local(): lax.psum((local_one, local_two, local_gain, local_bias), ('space', 'dp'))  245 us
    conv_general_dilated x2, matrix products, kernel_grad(): lax.conv_general_dilated(padded, target, (1, 1, 1), ((0, 0), (1, 1), (1,...  128 us
    psum x1, blocking collectives, local(): lax.psum((local_one, local_two, local_gain, local_bias), ('space', 'dp'))  101 us
    conv_general_dilated x3, matrix products, conv_slab(): lax.conv_general_dilated(padded, kernel, (1, 1, 1), ((0, 0), (1, 1), (1,...  39 us
    unnamed x46, local copies, waits for them, and re-layouts  36.6 us
    psum x1, blocking collectives, local(): lax.psum((jnp.sum(pre_act, axis=axes_cells, keepdims=True), jnp.sum(pre_a...  30.8 us
    psum x1, blocking collectives, local(): lax.psum((jnp.sum(grad_norm, axis=axes_cells, keepdims=True), jnp.sum(gra...  25 us
    concatenate x8, local copies, waits for them, and re-layouts, padded_2(): jnp.concatenate([lax.ppermute(tail, axis, [(i, (i + 1) % count) for i in...  20 us
  transfers between devices with their start and end apart: 9, of which 1 were waited for; matrix products, arithmetic and copies ran while one was open for 12% of the time, Pallas kernels for 0%

commit v1 on v0

--- a/solution.py
+++ b/solution.py
@@ -4,6 +4,11 @@
 from jax.sharding import PartitionSpec as P
 
 epsilon = 1e-05
+
+
+def axis_by_axis(array, first, second):
+    partial = lax.psum(array, first)
+    return lax.psum(partial, second)
 
 
 def padded_2(cells, sides, width):
@@ -97,8 +102,8 @@
     local_one = kernel_grad(padded_x, grad_pre)
     back = conv_slab(padded_grad, flipped(weight_one))
     grad_input = (upstream.astype(jnp.float32) + back).astype(jnp.bfloat16)
-    grad_one, grad_two, grad_gain, grad_bias = lax.psum(
-        (local_one, local_two, local_gain, local_bias), ("space", "dp")
+    grad_one, grad_two, grad_gain, grad_bias = axis_by_axis(
+        (local_one, local_two, local_gain, local_bias), "space", "dp"
     )
     return (grad_input, grad_one, grad_two, grad_gain, grad_bias)
 

time: 690 us -> 701 us (1.016)
  waiting for transfers between devices: 245 us -> 316 us
  matrix products: 167 us -> 130 us
  blocking collectives: 157 us -> 136 us
    psum x1 -> x2, waiting for transfers between devices: 245 us -> 316 us  [the longest x1 265 us: axis_by_axis(): return lax.psum(partial, second)]
    conv_general_dilated x2, matrix products: 128 us -> 91.3 us  [kernel_grad(): lax.conv_general_dilated(padded, target, (1, 1, 1), ((0, 0), (1, 1), (1,...]
    psum x1, blocking collectives: 101 us -> 79.9 us  [axis_by_axis(): return lax.psum(partial, second)]
    unnamed x46 -> x52, local copies, waits for them, and re-layouts: 36.6 us -> 34.2 us
  transfers between devices with their start and end apart: 9 -> 10, of which waited for: 1 -> 2; matrix products, arithmetic and copies ran while one was open for 12% -> 22% of each run, Pallas kernels for 0% -> 0%
where the time goes in v1:
time: 701 us; the launch traced here: 696 us
  waiting for transfers between devices  316 us (45%)
  blocking collectives  136 us (19%)
  matrix products  130 us (19%)
  local copies, waits for them, and re-layouts  66.4 us (9%)
  starting transfers between devices  21 us (3%)
  between operations  14.9 us (2%)
  other arithmetic  11.3 us (2%)
    psum x1, waiting for transfers between devices, axis_by_axis(): return lax.psum(partial, second)  265 us
    conv_general_dilated x2, matrix products, kernel_grad(): lax.conv_general_dilated(padded, target, (1, 1, 1), ((0, 0), (1, 1), (1,...  91.3 us
    psum x1, blocking collectives, axis_by_axis(): return lax.psum(partial, second)  79.9 us
    psum x1, waiting for transfers between devices, axis_by_axis(): partial = lax.psum(array, first)  51.7 us
    conv_general_dilated x3, matrix products, conv_slab(): lax.conv_general_dilated(padded, kernel, (1, 1, 1), ((0, 0), (1, 1), (1,...  38.6 us
    unnamed x52, local copies, waits for them, and re-layouts  34.2 us
    psum x1, blocking collectives, local(): lax.psum((jnp.sum(pre_act, axis=axes_cells, keepdims=True), jnp.sum(pre_a...  30.6 us
    psum x1, blocking collectives, local(): lax.psum((jnp.sum(grad_norm, axis=axes_cells, keepdims=True), jnp.sum(gra...  25.5 us
  transfers between devices with their start and end apart: 10, of which 2 were waited for; matrix products, arithmetic and copies ran while one was open for 22% of the time, Pallas kernels for 0%

profile of v1, /device:TPU:1, one launch (start us, length us, event | category | flops | bytes accessed | tf_op | source)
XLA Modules:
  0.0 695.7 jit_solution(1503938439072407728)
XLA Ops:
  7.2 1.0 fusion.73
  8.3 4.2 collective-permute-start
  12.5 1.3 collective-permute-start.1
  13.8 1.6 fusion.74
  15.4 4.6 collective-permute-start.2
  20.0 1.3 collective-permute-start.3
  21.3 7.4 %copy.112 = bf16[1,48,8,8,128]{1,0,4,3,2:T(2,128)(2,1)} copy(bf16[1,48,8,8,128]{4,3,2,1,0:T(8,128)(2,1)} %param.7) | data formatting | bytes 1572864 | tf_op args[1]
  28.7 2.6 copy.85
  31.3 3.5 copy.86
  34.8 3.6 fusion.70
  38.4 3.2 fusion.68
  42.1 1.5 copy-done.9
  43.6 0.8 slice.50
  44.5 2.0 pad_maximum_fusion.3
  46.5 5.1 copy.89
  51.6 2.3 pad.2
  54.5 0.8 slice.51
  55.3 1.2 copy-done.10
  56.9 12.2 %select_reduce_fusion.3 = (f32[48]{0:T(128)S(1)}, f32[48]{0:T(128)S(1)}, f32[8,8,8,17,48]{4,2,3,1,0:T(8,128)}) fusion(pred[8,17]{0,1:T(8,128)(4,1)S(1)} %copy-done.14, bf16[48,48,3,3,3]{1,0,4,3,2:T(8,128)(2,1)S(1)} %copy-done, bf16[48,10,8,1,7,2]{0,4,5,2,1,3:T(8,128)(2,1)S(1)} %copy-done.13, bf16[48,10,8,1,8,17]{0,4,5,2,1,3:T(8,128)(2,1)S(1)} %copy-done.10), kind=kOutput, calls=%fused_computation.25 | convolution fusion | flops 998682496 | bytes 2948104 | tf_op jit(solution)/shard_map/conv_general_dilated | solution.py:36
  69.0 30.6 %all-reduce.3 = (f32[1,48,1,1,1]{1,4,3,2,0:T(1,128)S(1)}, f32[1,48,1,1,1]{1,4,3,2,0:T(1,128)S(1)}) all-reduce(f32[1,48,1,1,1]{1,4,3,2,0:T(1,128)S(1)} %bitcast.112, f32[1,48,1,1,1]{1,4,3,2,0:T(1,128)S(1)} %bitcast.111), channel_id=1, replica_groups=mesh['space'=8,'dp'=32] {'space'}, use_global_device_ids=true, to_apply=%region_1.0 | all-reduce | flops 96 | bytes 768 | tf_op jit(solution)/shard_map/psum | solution.py:68
  99.6 16.4 %select_reduce_fusion = (f32[48]{0:T(128)S(1)}, f32[48]{0:T(128)S(1)}, f32[8,8,8,17,48]{4,2,3,1,0:T(8,128)}) fusion(pred[8,17]{0,1:T(8,128)(4,1)S(1)} %copy-done.14, f32[48]{0:T(128)S(1)} %bitcast.107, f32[48]{0:T(128)S(1)} %get-tuple-element.59, f32[8,8,8,17,48]{4,2,3,1,0:T(8,128)} %get-tuple-element.60, f32[48]{0:T(128)S(1)} %copy-done.17, ...), kind=kOutput, calls=%fused_computation.17 | convolution fusion | flops 1004113792 | bytes 4620040 | tf_op jit(solution)/shard_map/conv_general_dilated | solution.py:36
  116.0 25.5 %all-reduce.2 = (f32[1,48,1,1,1]{1,4,3,2,0:T(1,128)S(1)}, f32[1,48,1,1,1]{1,4,3,2,0:T(1,128)S(1)}, f32[48]{0:T(128)}, f32[48]{0:T(128)}) all-reduce(f32[1,48,1,1,1]{1,4,3,2,0:T(1,128)S(1)} %bitcast.110, f32[1,48,1,1,1]{1,4,3,2,0:T(1,128)S(1)} %bitcast.109, f32[48]{0:T(128)S(1)} %get-tuple-element.25, ...), channel_id=1, replica_groups=mesh['space'=8,'dp'=32] {'space'}, use_global_device_ids=true, to_apply=%region_5.0 | all-reduce | flops 192 | bytes 1536 | tf_op jit(solution)/shard_map/psum | solution.py:89
  141.5 4.9 multiply_convert_fusion.1
  146.4 1.7 copy.93
  148.3 1.2 copy.128
  149.5 2.1 collective-permute-start.6
  151.6 1.2 copy.127
  152.8 1.3 collective-permute-start.7
  154.1 2.3 copy.117
  156.4 2.3 copy.118
  158.8 1.9 copy.104
  161.5 4.7 collective-permute-start.4
  167.0 1.5 collective-permute-start.5
  168.5 1.6 fusion.36
  170.1 16.3 %fusion.49 = f32[48,48,3,3,3]{0,1,4,3,2:T(8,128)} fusion(bf16[8,8,8,17,48]{4,2,3,1,0:T(8,128)(2,1)S(1)} %get-tuple-element.44, pred[8,17]{0,1:T(8,128)(4,1)S(1)} %copy-done.14, bf16[48,10,8,8,17,1]{0,3,5,4,2,1:T(8,128)(2,1)S(1)} %get-tuple-element.64, bf16[48,10,8,8,17,1]{0,3,5,4,2,1:T(8,128)(2,1)S(1)} %copy-done.11, ...), kind=kOutput, calls=%fused_computation.61 | convolution fusion | flops 1002491904 | bytes 4217992 | tf_op jit(solution)/shard_map/conv_general_dilated | solution.py:51
  186.8 6.3 copy.126
  193.2 75.0 %fusion.11 = f32[48,48,3,3,3]{0,1,4,3,2:T(8,128)} fusion(bf16[1,48,8,8,128]{1,0,4,3,2:T(2,128)(2,1)S(1)} %copy-done.7, bf16[1,48,1,8,128]{1,0,4,3,2:T(2,128)(2,1)} %collective-permute-done.7, bf16[1,48,8,8,128]{1,0,4,3,2:T(2,128)(2,1)} %bitcast.102, bf16[1,48,1,8,128]{1,0,4,3,2:T(2,128)(2,1)} %collective-permute-done.6), kind=kOutput, calls=%fused_computation.15 | convolution fusion | flops 932364288 | bytes 2018304 | tf_op jit(solution)/shard_map/conv_general_dilated | solution.py:51
  268.3 1.5 slice_bitcast_fusion.1
  269.8 79.9 %all-reduce = (f32[48]{0:T(128)}, f32[48]{0:T(128)}) all-reduce(f32[48]{0:T(128)S(1)} %copy-done.18, f32[48]{0:T(128)S(1)} %copy-done.19), channel_id=1, replica_groups=mesh['space'=8,'dp'=32] {'dp'}, use_global_device_ids=true, to_apply=%region_13.0 | all-reduce | flops 96 | bytes 768 | tf_op jit(solution)/shard_map/psum | solution.py:11
  349.7 2.3 maximum_bitcast_fusion
  353.1 51.7 %all-reduce.10.cloned.1.call-done = (f32[48,48,3,3,3]{0,1,4,3,2:T(8,128)}, f32[48,48,3,3,3]{0,1,4,3,2:T(8,128)}) async-done(((f32[48,48,3,3,3]{0,1,4,3,2:T(8,128)}, f32[48,48,3,3,3]{0,1,4,3,2:T(8,128)}), (f32[48,48,3,3,3]{0,1,4,3,2:T(8,128)}, f32[48,48,3,3,3]{0,1,4,3,2:T(8,128)})) %all-reduce.10.cloned.1.call-update) | async-done | bytes 497680 | tf_op jit(solution)/shard_map/psum | solution.py:10
  404.8 10.1 %broadcast_select_fusion = f32[8,8,8,17,48]{4,2,3,1,0:T(8,128)S(1)} fusion(pred[8,17]{0,1:T(8,128)(4,1)S(1)} %copy-done.15, bf16[48,48,3,3,3]{1,0,4,3,2:T(8,128)(2,1)S(1)} %copy-done, bf16[48,10,8,1,7,2]{0,4,5,2,1,3:T(8,128)(2,1)S(1)} %slice.57, bf16[48,10,8,1,8,17]{0,4,5,2,1,3:T(8,128)(2,1)S(1)} %copy.98), kind=kOutput, calls=%fused_computation.55 | convolution fusion | flops 996593664 | bytes 2947720 | tf_op jit(solution)/shard_map/conv_general_dilated | solution.py:36
  414.9 0.8 copy.99
  415.7 0.8 copy-done.4
  416.9 2.7 copy.113
  419.6 264.5 %all-reduce.8.cloned.1.call-done = (f32[48,48,3,3,3]{0,1,4,3,2:T(8,128)}, f32[48,48,3,3,3]{0,1,4,3,2:T(8,128)}) async-done(((f32[48,48,3,3,3]{0,1,4,3,2:T(8,128)}, f32[48,48,3,3,3]{0,1,4,3,2:T(8,128)}), (f32[48,48,3,3,3]{0,1,4,3,2:T(8,128)}, f32[48,48,3,3,3]{0,1,4,3,2:T(8,128)})) %all-reduce.8.cloned.1.call-update) | async-done | bytes 497680 | tf_op jit(solution)/shard_map/psum | solution.py:11
  684.1 2.2 copy.114
  686.3 2.2 copy.115
  (73 shorter events, 5.4 us)
Async XLA Ops:
  7.2 48.2 %copy-start = (bf16[48,48,3,3,3]{1,0,4,3,2:T(8,128)(2,1)S(1)}, bf16[48,48,3,3,3]{1,0,4,3,2:T(8,128)(2,1)}, u32[]{:S(2)}) copy-start(bf16[48,48,3,3,3]{1,0,4,3,2:T(8,128)(2,1)} %param.8) | copy-start | bytes 373252
  7.2 21.5 %copy-start.5 = (bf16[1,48,8,8,128]{4,3,2,1,0:T(8,128)(2,1)S(1)}, bf16[1,48,8,8,128]{4,3,2,1,0:T(8,128)(2,1)}, u32[]{:S(2)}) copy-start(bf16[1,48,8,8,128]{4,3,2,1,0:T(8,128)(2,1)} %param.7) | copy-start | bytes 2359300
  7.2 397.6 %all-reduce.10.cloned.1.call-start = ((), (), s32[]{:S(2)}) async-start(), calls=%async_computation.1 | async-start | bytes 2654208 | tf_op jit(solution)/shard_map/psum | solution.py:10
  8.3 22.9 %copy-start.12 = (bf16[1,48,8,8,128]{4,3,2,1,0:T(8,128)(2,1)S(1)}, bf16[1,48,8,8,128]{4,3,2,1,0:T(8,128)(2,1)}, u32[]{:S(2)}) copy-start(bf16[1,48,8,8,128]{4,3,2,1,0:T(8,128)(2,1)} %param.6) | copy-start | bytes 2359300
  8.3 22.9 %collective-permute-start = (bf16[1,48,1,8,128]{4,3,2,1,0:T(8,128)(2,1)S(1)}, bf16[1,48,1,8,128]{4,3,2,1,0:T(8,128)(2,1)S(1)}, u32[]{:S(2)}, u32[]{:S(2)}) collective-permute-start(bf16[1,48,1,8,128]{4,3,2,1,0:T(8,128)(2,1)S(1)} %get-tuple-element.55), channel_id=1, source_target_pairs={{0,32},{32,64},{64,96},{96,128},{128,160},{160,192},{192,224},{1,3... | collective-permute-start | bytes 294920 | tf_op jit(solution)/shard_map/ppermute | solution.py:22
  12.5 18.7 %collective-permute-start.1 = (bf16[1,48,1,8,128]{4,3,2,1,0:T(8,128)(2,1)S(1)}, bf16[1,48,1,8,128]{4,3,2,1,0:T(8,128)(2,1)S(1)}, u32[]{:S(2)}, u32[]{:S(2)}) collective-permute-start(bf16[1,48,1,8,128]{4,3,2,1,0:T(8,128)(2,1)S(1)} %get-tuple-element.56), channel_id=1, source_target_pairs={{32,0},{64,32},{96,64},{128,96},{160,128},{192,160},{224,192},{33,... | collective-permute-start | bytes 294920 | tf_op jit(solution)/shard_map/ppermute | solution.py:24
  15.4 29.1 %collective-permute-start.2 = (bf16[1,48,1,8,128]{4,3,2,1,0:T(8,128)(2,1)}, bf16[1,48,1,8,128]{4,3,2,1,0:T(8,128)(2,1)}, u32[]{:S(2)}, u32[]{:S(2)}) collective-permute-start(bf16[1,48,1,8,128]{4,3,2,1,0:T(8,128)(2,1)} %get-tuple-element.57), channel_id=1, source_target_pairs={{0,32},{32,64},{64,96},{96,128},{128,160},{160,192},{192,224},{1,3... | collective-permute-start | bytes 294920 | tf_op jit(solution)/shard_map/ppermute | solution.py:22
  20.0 24.5 %collective-permute-start.3 = (bf16[1,48,1,8,128]{4,3,2,1,0:T(8,128)(2,1)S(1)}, bf16[1,48,1,8,128]{4,3,2,1,0:T(8,128)(2,1)}, u32[]{:S(2)}, u32[]{:S(2)}) collective-permute-start(bf16[1,48,1,8,128]{4,3,2,1,0:T(8,128)(2,1)S(1)} %get-tuple-element.58), channel_id=1, source_target_pairs={{32,0},{64,32},{96,64},{128,96},{160,128},{192,160},{224,192},{33,... | collective-permute-start | bytes 294920 | tf_op jit(solution)/shard_map/ppermute | solution.py:24
  41.6 2.9 copy-start.6
  42.1 1.5 copy-start.9
  54.0 2.6 copy-start.10
  54.0 2.8 copy-start.13
  54.0 2.8 copy-start.14
  54.5 14.5 %copy-start.8 = (bf16[48,10,8,1,8,17]{0,4,5,2,1,3:T(8,128)(2,1)}, bf16[48,10,8,1,8,17]{0,4,5,2,1,3:T(8,128)(2,1)S(1)}, u32[]{:S(2)}) copy-start(bf16[48,10,8,1,8,17]{0,4,5,2,1,3:T(8,128)(2,1)S(1)} %copy.91) | copy-start | bytes 3133444
  56.9 42.8 %copy-start.16 = (f32[48]{0:T(128)S(1)}, f32[48]{0:T(128)}, u32[]{:S(2)}) copy-start(f32[48]{0:T(128)} %param.10) | copy-start | bytes 580
  56.9 42.8 %copy-start.17 = (f32[48]{0:T(128)S(1)}, f32[48]{0:T(128)}, u32[]{:S(2)}) copy-start(f32[48]{0:T(128)} %param.11) | copy-start | bytes 580
  146.4 7.7 %copy-start.2 = (bf16[48,10,8,1,8,16]{0,2,5,4,1,3:T(8,128)(2,1)S(1)}, bf16[48,10,8,1,8,16]{0,2,5,4,1,3:T(8,128)(2,1)}, u32[]{:S(2)}) copy-start(bf16[48,10,8,1,8,16]{0,2,5,4,1,3:T(8,128)(2,1)} %get-tuple-element.45) | copy-start | bytes 2949124
  148.2 8.2 %copy-start.1 = (bf16[48,10,8,1,8,16]{0,2,5,4,1,3:T(8,128)(2,1)S(1)}, bf16[48,10,8,1,8,16]{0,2,5,4,1,3:T(8,128)(2,1)}, u32[]{:S(2)}) copy-start(bf16[48,10,8,1,8,16]{0,2,5,4,1,3:T(8,128)(2,1)} %get-tuple-element.46) | copy-start | bytes 2949124
  149.5 43.7 %collective-permute-start.6 = (bf16[1,48,1,8,128]{1,0,4,3,2:T(2,128)(2,1)}, bf16[1,48,1,8,128]{1,0,4,3,2:T(2,128)(2,1)}, u32[]{:S(2)}, u32[]{:S(2)}) collective-permute-start(bf16[1,48,1,8,128]{1,0,4,3,2:T(2,128)(2,1)} %bitcast.90), channel_id=1, source_target_pairs={{0,32},{32,64},{64,96},{96,128},{128,160},{160,192},{192,224},{1,3... | collective-permute-start | bytes 294920 | tf_op jit(solution)/shard_map/ppermute | solution.py:22
  152.8 40.3 %collective-permute-start.7 = (bf16[1,48,1,8,128]{1,0,4,3,2:T(2,128)(2,1)}, bf16[1,48,1,8,128]{1,0,4,3,2:T(2,128)(2,1)}, u32[]{:S(2)}, u32[]{:S(2)}) collective-permute-start(bf16[1,48,1,8,128]{1,0,4,3,2:T(2,128)(2,1)} %bitcast.89), channel_id=1, source_target_pairs={{32,0},{64,32},{96,64},{128,96},{160,128},{192,160},{224,192},{33,... | collective-permute-start | bytes 294920 | tf_op jit(solution)/shard_map/ppermute | solution.py:24
  161.5 188.2 %collective-permute-start.4 = (bf16[1,48,1,8,128]{1,3,4,0,2:T(8,128)(2,1)}, bf16[1,48,1,8,128]{1,3,4,0,2:T(8,128)(2,1)}, u32[]{:S(2)}, u32[]{:S(2)}) collective-permute-start(bf16[1,48,1,8,128]{1,3,4,0,2:T(8,128)(2,1)} %slice_bitcast_fusion.3), channel_id=1, source_target_pairs={{0,32},{32,64},{64,96},{96,128},{128,160},{160,192},{192,224},{1,3... | collective-permute-start | bytes 294920 | tf_op jit(solution)/shard_map/ppermute | solution.py:22
  167.0 3.1 copy-start.11
  167.0 182.7 %collective-permute-start.5 = (bf16[1,48,1,8,128]{1,3,4,2,0:T(8,128)(2,1)}, bf16[1,48,1,8,128]{1,3,4,2,0:T(8,128)(2,1)}, u32[]{:S(2)}, u32[]{:S(2)}) collective-permute-start(bf16[1,48,1,8,128]{1,3,4,2,0:T(8,128)(2,1)} %slice_bitcast_fusion.2), channel_id=1, source_target_pairs={{32,0},{64,32},{96,64},{128,96},{160,128},{192,160},{224,192},{33,... | collective-permute-start | bytes 294920 | tf_op jit(solution)/shard_map/ppermute | solution.py:24
  186.8 6.3 copy-start.7
  193.2 75.1 %copy-start.3 = (bf16[8,8,8,17,48]{4,1,3,2,0:T(8,128)(2,1)S(1)}, bf16[8,8,8,17,48]{4,1,3,2,0:T(8,128)(2,1)}, u32[]{:S(2)}) copy-start(bf16[8,8,8,17,48]{4,1,3,2,0:T(8,128)(2,1)} %copy.93) | copy-start | bytes 2506756
  268.2 1.6 copy-start.18
  268.2 1.6 copy-start.19
  268.2 415.9 %all-reduce.8.cloned.1.call-start = ((), (), s32[]{:S(2)}) async-start(), calls=%async_computation | async-start | bytes 2654208 | tf_op jit(solution)/shard_map/psum | solution.py:11
  352.5 52.3 %copy-start.15 = (pred[8,17]{0,1:T(8,128)(4,1)S(1)}, pred[8,17]{0,1:T(8,128)(4,1)}, u32[]{:S(2)}) copy-start(pred[8,17]{0,1:T(8,128)(4,1)} %constant.35) | copy-start | bytes 412
  414.9 1.6 copy-start.4
Sparse Core Ops, SparseCore 0:
  268.3 136.3 all-reduce.9
  407.7 276.3 all-reduce.7
